TPU v7x, 128 devices: a whole 4x4x4 slice. The times are simulated.
128 devices in a mesh: gx: 32 (over y, z, core), gy: 4 (over x).
Axes of the slice: x: 4, y: 4, z: 4, core: 2. Of those that a mesh axis runs over, the one named last changes fastest.
Arguments:
- right_side: float32 [4, 24, 768, 512], P(None, None, 'gx', 'gy'), may hold values from -8 to 8
- start_field: float32 [4, 24, 768, 512], P(None, None, 'gx', 'gy'), may hold values from -4 to 4
- center: float32 [24, 768, 512], P(None, 'gx', 'gy'), may hold values from 0.5 to 3
- weights: float32 [6, 24, 768, 512], P(None, None, 'gx', 'gy'), may hold values from 0.4 to 1.4
Outputs:
- solution: float32 [4, 24, 768, 512], P(None, None, 'gx', 'gy')
- residual: float32 [4, 24, 768, 512], P(None, None, 'gx', 'gy')
All inputs are finite; a program needn't handle non-finite values.
Results may differ from a plain program's by a relative error of at most 0.0033.
Values sent between devices are 32-bit elements; how exact they have to be, the bound alone decides.
A program may use at most 128 MiB of HBM per device.

v0:
```python
import functools

import jax
import jax.numpy as jnp
from jax import lax
from jax.experimental import pallas as pl
from jax.experimental.pallas import tpu as pltpu
from jax.sharding import PartitionSpec as P

SHIFTS = (12.0, 2.0, 8.0, 5.0)
SCALE_DOWN = 5.0
MESH = pl.DeviceIdType.MESH

R, NZ, BX, L = 4, 24, 24, 128
XT = BX // 8
FR = R * NZ * BX
WR = NZ * BX
PAD = 24
FS = FR + 2 * PAD


def pair_table():
    table, groups, at = {}, [], 0
    for level in range(4):
        for other in (level, 4) + tuple(range(level)):
            pairs = [
                (a, b)
                for a in range(R)
                for b in range(R)
                if other != level or b <= a
            ]
            for index, (a, b) in enumerate(pairs):
                table[(level, a, other, b)] = at + index
            groups.append((level, other, at, pairs))
            at += (len(pairs) + 7) // 8 * 8
    return table, groups, at


TABLE, GROUPS, USED = pair_table()
LANES = 256


def kernel(
    gx_size, gy_size, inner,
    b_hbm, x0_hbm, c_hbm, w_hbm,
    sol, res,
    F, W, B, C6, WM, WE, WX, HX, HY, XS, YS, HC, ACC, RED, RA, RB, CS,
    ld, sx, rx, sy, ry, sa, ra, sb, rb,
):
    gx = lax.axis_index("gx")
    gy = lax.axis_index("gy")
    outer = gx_size // inner
    base_x = (gx // inner) * inner
    in_x = gx - base_x

    loads = [
        pltpu.make_async_copy(x0_hbm, F.at[pl.ds(PAD, FR)], ld.at[0]),
        pltpu.make_async_copy(w_hbm, WM, ld.at[1]),
        pltpu.make_async_copy(c_hbm, C6, ld.at[2]),
        pltpu.make_async_copy(b_hbm, B, ld.at[3]),
    ]
    for copy in loads:
        copy.start()

    barrier = pltpu.get_barrier_semaphore()
    hello = []
    for step in (1, gx_size - 1):
        hello.append((lax.rem(gx + step, gx_size), gy))
    for step in (1, gy_size - 1):
        hello.append((gx, lax.rem(gy + step, gy_size)))
    inner_peers = [(base_x + lax.rem(in_x + i, inner), gy) for i in range(1, inner)]
    outer_peers = []
    for i in range(outer):
        for j in range(gy_size):
            if i or j:
                outer_peers.append(
                    (lax.rem(gx + i * inner, gx_size), lax.rem(gy + j, gy_size))
                )
    for peer in hello + inner_peers + outer_peers:
        pl.semaphore_signal(barrier, inc=1, device_id=peer, device_id_type=MESH)

    zero = jnp.zeros((8, L), jnp.float32)
    lane = lax.broadcasted_iota(jnp.int32, (8, L), 1)
    sub = lax.broadcasted_iota(jnp.int32, (8, L), 0)
    first_x, last_x = gx == 0, gx == gx_size - 1
    first_y, last_y = gy == 0, gy == gy_size - 1
    for f in range(5):
        for p in range(3):
            F[pl.ds(f * FS + 8 * p, 8), :] = zero
            F[pl.ds(f * FS + PAD + FR + 8 * p, 8), :] = zero

    def clear(ref, level, side):
        rows = ref.shape[2]
        for q in range(rows // 8):
            ref[level, side, pl.ds(8 * q, 8), :] = zero

    for cond, ref, side in (
        (first_x, HX, 0), (last_x, HX, 1), (first_y, HY, 0), (last_y, HY, 1),
    ):
        @pl.when(cond)
        def _(ref=ref, side=side):
            for level in range(5):
                clear(ref, level, side)

    def pack_masks(z):
        masks = []
        for half in range(2):
            j2 = 2 * (half * NZ + z)
            masks.append((((lane + 1 - j2) & (L - 1)) < 2, j2))
        return masks

    def tile_row(r, z, xt):
        return (r * NZ + z) * BX + 8 * xt

    def pack_tile(tile, r, xt, masks, acc):
        mask, j2 = masks[r % 2]
        at = (r // 2) * XT + xt
        acc[at] = jnp.where(mask, pltpu.roll(tile, j2, 1), acc[at])

    def store_packed(acc):
        for q in range(2 * XT):
            YS[pl.ds(8 * q, 8), :] = acc[q]

    def copies_x(level):
        return (
            (last_x, pltpu.make_async_remote_copy(
                src_ref=XS.at[level, 1], dst_ref=HX.at[level, 0],
                send_sem=sx.at[level, 1], recv_sem=rx.at[level, 0],
                device_id=(gx + 1, gy), device_id_type=MESH)),
            (first_x, pltpu.make_async_remote_copy(
                src_ref=XS.at[level, 0], dst_ref=HX.at[level, 1],
                send_sem=sx.at[level, 0], recv_sem=rx.at[level, 1],
                device_id=(gx - 1, gy), device_id_type=MESH)),
        )

    def copies_y(level):
        return (
            (last_y, pltpu.make_async_remote_copy(
                src_ref=YS, dst_ref=HY.at[level, 0],
                send_sem=sy.at[level, 1], recv_sem=ry.at[level, 0],
                device_id=(gx, gy + 1), device_id_type=MESH)),
            (first_y, pltpu.make_async_remote_copy(
                src_ref=YS, dst_ref=HY.at[level, 1],
                send_sem=sy.at[level, 0], recv_sem=ry.at[level, 1],
                device_id=(gx, gy - 1), device_id_type=MESH)),
        )

    def send(level, acc):
        store_packed(acc)
        for cond, copy in copies_y(level):
            @pl.when(jnp.logical_not(cond))
            def _(copy=copy):
                copy.start()
        for side, row in ((0, 0), (1, BX - 1)):
            for r in range(R):
                rows = F[pl.ds(level * FS + PAD + r * WR + row, NZ, stride=BX), :]
                XS[level, side, pl.ds(r * NZ, NZ), :] = rows
        for cond, copy in copies_x(level):
            @pl.when(jnp.logical_not(cond))
            def _(copy=copy):
                copy.start()

    def receive(level):
        for cond, (_, copy) in (
            (first_x, copies_x(level)[0]), (last_x, copies_x(level)[1]),
            (first_y, copies_y(level)[0]), (last_y, copies_y(level)[1]),
        ):
            @pl.when(jnp.logical_not(cond))
            def _(copy=copy):
                copy.wait_recv()
        for cond, copy in copies_x(level) + copies_y(level):
            @pl.when(jnp.logical_not(cond))
            def _(copy=copy):
                copy.wait_send()

    def bulk(level):
        base = level * FS + PAD
        out = max(level - 1, 0) * FR

        def body(z, carry):
            for xt in range(XT):
                wrow = pl.multiple_of(z * BX + 8 * xt, 8)
                w = [WM[pl.ds(k * WR + wrow, 8), :] for k in range(6)]
                c6 = C6[pl.ds(wrow, 8), :]
                for r in range(R):
                    row = pl.multiple_of(tile_row(r, z, xt), 8)
                    at = base + row
                    mid = F[pl.ds(at, 8), :]
                    beside = w[0] * F[pl.ds(at - 1, 8), :] + w[1] * F[pl.ds(at + 1, 8), :]
                    beside = beside + w[2] * pltpu.roll(mid, 1, 1) + w[3] * pltpu.roll(mid, L - 1, 1)
                    beside = beside + w[4] * F[pl.ds(at - BX, 8), :] + w[5] * F[pl.ds(at + BX, 8), :]
                    W[pl.ds(out + row, 8), :] = c6 * mid - beside
            return carry

        lax.fori_loop(0, NZ, body, 0)

    def correct(level):
        out = max(level - 1, 0) * FR
        for side, row in ((0, 0), (1, BX - 1)):
            for r in range(R):
                where = pl.ds(out + r * WR + row, NZ, stride=BX)
                W[where, :] = W[where, :] - (
                    WX[pl.ds(side * NZ, NZ), :] * HX[level, side, pl.ds(r * NZ, NZ), :]
                )
        even = (lane & 1) == 0
        for q in range(2 * XT):
            HC[pl.ds(8 * q, 8), :] = jnp.where(
                even,
                pltpu.roll(HY[level, 0, pl.ds(8 * q, 8), :], 1, 1),
                pltpu.roll(HY[level, 1, pl.ds(8 * q, 8), :], L - 1, 1),
            )

        def body(z, acc):
            acc = list(acc)
            masks = pack_masks(z)
            for xt in range(XT):
                edge = WE[pl.ds(pl.multiple_of(z * BX + 8 * xt, 8), 8), :]
                for r in range(R):
                    row = pl.multiple_of(tile_row(r, z, xt), 8)
                    halo = HC[pl.ds(8 * ((r // 2) * XT + xt), 8), :]
                    halo = pltpu.roll(halo, lax.rem(L - masks[r % 2][1], L), 1)
                    image = W[pl.ds(out + row, 8), :] - edge * halo
                    if level == 0:
                        following = B[pl.ds(row, 8), :] - image
                    else:
                        W[pl.ds(out + row, 8), :] = image
                        held = F[pl.ds(level * FS + PAD + row, 8), :]
                        following = (image - SHIFTS[level - 1] * held) * (1.0 / SCALE_DOWN)
                    if level < 4:
                        F[pl.ds((level + 1) * FS + PAD + row, 8), :] = following
                        pack_tile(following, r, xt, masks, acc)
            return tuple(acc)

        return lax.fori_loop(0, NZ, body, (zero,) * (2 * XT))

    def combine(a, b, d):
        mask = (sub & d) == 0
        return jnp.where(mask, a, b) + pltpu.roll(jnp.where(mask, b, a), d, 0)

    def gram(level):
        for lev, other, start, pairs in GROUPS:
            if lev != level:
                continue

            def rows_of(block, r, z, xt):
                row = pl.multiple_of(tile_row(r, z, xt), 8)
                if block == 4:
                    return F[pl.ds(FS + PAD + row, 8), :]
                return W[pl.ds(block * FR + row, 8), :]

            def body(z, acc):
                acc = list(acc)
                for xt in range(XT):
                    left = [rows_of(lev, r, z, xt) for r in range(R)]
                    right = left
                    if other != lev:
                        right = [rows_of(other, r, z, xt) for r in range(R)]
                    for index, (a, b) in enumerate(pairs):
                        acc[index] = acc[index] + left[a] * right[b]
                return tuple(acc)

            sums = list(lax.fori_loop(0, NZ, body, (zero,) * len(pairs)))
            sums += [zero] * (-len(sums) % 8)
            for q in range(0, len(sums), 8):
                part = sums[q : q + 8]
                for d in (1, 2, 4):
                    part = [combine(part[k], part[k + 1], d) for k in range(0, len(part), 2)]
                RED[pl.ds(start + q, 8), :] = part[0]

    loads[0].wait()

    def pack_body(z, acc):
        acc = list(acc)
        masks = pack_masks(z)
        for xt in range(XT):
            for r in range(R):
                row = pl.multiple_of(tile_row(r, z, xt), 8)
                pack_tile(F[pl.ds(PAD + row, 8), :], r, xt, masks, acc)
        return tuple(acc)

    acc = lax.fori_loop(0, NZ, pack_body, (zero,) * (2 * XT))
    pl.semaphore_wait(barrier, len(hello) + len(inner_peers) + len(outer_peers))
    send(0, acc)

    loads[1].wait()
    loads[2].wait()
    WX[pl.ds(0, NZ), :] = WM[pl.ds(0, NZ, stride=BX), :]
    WX[pl.ds(NZ, NZ), :] = WM[pl.ds(WR + BX - 1, NZ, stride=BX), :]

    def prepare(z, carry):
        for xt in range(XT):
            row = pl.multiple_of(z * BX + 8 * xt, 8)
            C6[pl.ds(row, 8), :] = C6[pl.ds(row, 8), :] + 6.0
            if xt == 0:
                WM[pl.ds(row, 8), :] = jnp.where(sub == 0, 0.0, WM[pl.ds(row, 8), :])
            if xt == XT - 1:
                at = WR + row
                WM[pl.ds(at, 8), :] = jnp.where(sub == 7, 0.0, WM[pl.ds(at, 8), :])
            low = WM[pl.ds(2 * WR + row, 8), :]
            high = WM[pl.ds(3 * WR + row, 8), :]
            WE[pl.ds(row, 8), :] = jnp.where(
                lane == 0, low, jnp.where(lane == L - 1, high, 0.0)
            )
            WM[pl.ds(2 * WR + row, 8), :] = jnp.where(lane == 0, 0.0, low)
            WM[pl.ds(3 * WR + row, 8), :] = jnp.where(lane == L - 1, 0.0, high)
        return carry

    lax.fori_loop(0, NZ, prepare, 0)
    for xt in range(XT):
        WM[pl.ds(4 * WR + 8 * xt, 8), :] = zero
        WM[pl.ds(5 * WR + (NZ - 1) * BX + 8 * xt, 8), :] = zero
    bulk(0)
    loads[3].wait()
    receive(0)
    acc = correct(0)
    for level in range(1, 5):
        send(level, acc)
        bulk(level)
        if level >= 2:
            gram(level - 2)
        receive(level)
        acc = correct(level)
    gram(3)

    for q in range(USED, LANES, 8):
        RED[pl.ds(q, 8), :] = zero
    total = lax.dot_general(
        jnp.ones((8, L), jnp.float32), RED[...], (((1,), (1,)), ((), ())),
        precision=lax.Precision.HIGHEST, preferred_element_type=jnp.float32,
    )

    def exchange(total, buffer, peers, send_sems, recv_sems):
        buffer[0] = total
        copies = []
        for k, peer in enumerate(peers):
            copy = pltpu.make_async_remote_copy(
                src_ref=buffer.at[0], dst_ref=buffer.at[k + 1],
                send_sem=send_sems.at[k], recv_sem=recv_sems.at[k],
                device_id=peer, device_id_type=MESH,
            )
            copy.start()
            copies.append(copy)
        for copy in copies:
            copy.wait_recv()
        parts = [buffer[k] for k in range(len(peers) + 1)]
        while len(parts) > 1:
            parts = [
                parts[k] + parts[k + 1] if k + 1 < len(parts) else parts[k]
                for k in range(0, len(parts), 2)
            ]
        for copy in copies:
            copy.wait_send()
        return parts[0]

    total = exchange(total, RA, inner_peers, sa, ra)
    total = exchange(total, RB, outer_peers, sb, rb)

    def entry(p):
        block = total[:, (p // L) * L : (p // L + 1) * L]
        return jnp.broadcast_to(block[:, p % L : p % L + 1], (8, L))

    order = 16
    A = {}
    for i in range(order):
        for j in range(i + 1):
            A[i, j] = entry(TABLE[(i // R, i % R, j // R, j % R)])
    rhs = []
    for i in range(order):
        column = [entry(TABLE[(i // R, i % R, 4, r)]) for r in range(R)]
        rhs.append(
            jnp.where(sub == 0, column[0],
                      jnp.where(sub == 1, column[1],
                                jnp.where(sub == 2, column[2], column[3])))
        )
    lower, inverse = {}, []
    for k in range(order):
        inv = 1.0 / A[k, k]
        inverse.append(inv)
        for i in range(k + 1, order):
            lower[i, k] = A[i, k] * inv
        for i in range(k + 1, order):
            for j in range(k + 1, i + 1):
                A[i, j] = A[i, j] - lower[i, k] * A[j, k]
            rhs[i] = rhs[i] - lower[i, k] * rhs[k]
    coeffs = [None] * order
    for k in range(order - 1, -1, -1):
        value = rhs[k] * inverse[k]
        for i in range(order - 1, k, -1):
            value = value - lower[i, k] * coeffs[i]
        coeffs[k] = value
        for r in range(R):
            CS[pl.ds((r * order + k) * 8, 8), :] = jnp.broadcast_to(value[r : r + 1], (8, L))

    for half in range(2):
        coef = [
            [CS[pl.ds(((2 * half + r) * order + k) * 8, 8), :] for k in range(order)]
            for r in range(2)
        ]

        def update(z, carry, half=half, coef=coef):
            for xt in range(XT):
                out = [pl.multiple_of(tile_row(2 * half + r, z, xt), 8) for r in range(2)]
                new_sol = [F[pl.ds(PAD + out[r], 8), :] for r in range(2)]
                new_res = [F[pl.ds(FS + PAD + out[r], 8), :] for r in range(2)]
                for k in range(order):
                    row = pl.multiple_of(tile_row(k % R, z, xt), 8)
                    basis = F[pl.ds((k // R + 1) * FS + PAD + row, 8), :]
                    image = W[pl.ds((k // R) * FR + row, 8), :]
                    for r in range(2):
                        new_sol[r] = new_sol[r] + coef[r][k] * basis
                        new_res[r] = new_res[r] - coef[r][k] * image
                for r in range(2):
                    sol[pl.ds(out[r], 8), :] = new_sol[r]
                    res[pl.ds(out[r], 8), :] = new_res[r]
            return carry

        lax.fori_loop(0, NZ, update, 0)


def on_device(gx_size, gy_size, right_side, start_field, center, weights):
    inner = min(8, gx_size // 2)
    outer = gx_size // inner
    dma = pltpu.SemaphoreType.DMA
    f32 = jnp.float32
    flat = lambda a: a.reshape(-1, L)
    out = pl.pallas_call(
        functools.partial(kernel, gx_size, gy_size, inner),
        out_shape=[jax.ShapeDtypeStruct((FR, L), f32)] * 2,
        in_specs=[pl.BlockSpec(memory_space=pltpu.HBM)] * 4,
        out_specs=[pl.BlockSpec(memory_space=pltpu.VMEM)] * 2,
        scratch_shapes=[
            pltpu.VMEM((5 * FS, L), f32),
            pltpu.VMEM((4 * FR, L), f32),
            pltpu.VMEM((FR, L), f32),
            pltpu.VMEM((WR, L), f32),
            pltpu.VMEM((6 * WR, L), f32),
            pltpu.VMEM((WR, L), f32),
            pltpu.VMEM((2 * NZ, L), f32),
            pltpu.VMEM((5, 2, R * NZ, L), f32),
            pltpu.VMEM((5, 2, 2 * BX, L), f32),
            pltpu.VMEM((5, 2, R * NZ, L), f32),
            pltpu.VMEM((2 * BX, L), f32),
            pltpu.VMEM((2 * BX, L), f32),
            pltpu.VMEM((8, L), f32),
            pltpu.VMEM((LANES, L), f32),
            pltpu.VMEM((inner, 8, LANES), f32),
            pltpu.VMEM((outer * gy_size, 8, LANES), f32),
            pltpu.VMEM((64 * 8, L), f32),
            dma((4,)),
            dma((5, 2)), dma((5, 2)), dma((5, 2)), dma((5, 2)),
            dma((inner,)), dma((inner,)),
            dma((outer * gy_size,)), dma((outer * gy_size,)),
        ],
        compiler_params=pltpu.CompilerParams(
            collective_id=0, has_side_effects=True, vmem_limit_bytes=48 * 1024 * 1024,
        ),
    )(flat(right_side), flat(start_field), flat(center), flat(weights))
    return tuple(o.reshape(R, NZ, BX, L) for o in out)


def solution(mesh):
    gx_size, gy_size = mesh.shape["gx"], mesh.shape["gy"]
    return jax.shard_map(
        functools.partial(on_device, gx_size, gy_size),
        mesh=mesh,
        in_specs=(
            P(None, None, "gx", "gy"),
            P(None, None, "gx", "gy"),
            P(None, "gx", "gy"),
            P(None, None, "gx", "gy"),
        ),
        out_specs=(P(None, None, "gx", "gy"), P(None, None, "gx", "gy")),
        check_vma=False,
    )
```

profile of v0, /device:TPU:1, one launch (start us, length us, event | category | flops | bytes accessed | tf_op | source)
XLA Modules:
  0.0 65.8 jit_solution(11701278051779143443)
XLA Ops:
  0.6 0.0 copy-start
  0.6 1.3 %copy-done = f32[4,24,24,128]{3,2,1,0:T(8,128)S(1)} copy-done((f32[4,24,24,128]{3,2,1,0:T(8,128)S(1)}, f32[4,24,24,128]{3,2,1,0:T(8,128)}, u32[]{:S(2)}) %copy-start) | copy-done | bytes 1179672
  1.9 0.0 copy-start.1
  1.9 1.3 %copy-done.1 = f32[4,24,24,128]{3,2,1,0:T(8,128)S(1)} copy-done((f32[4,24,24,128]{3,2,1,0:T(8,128)S(1)}, f32[4,24,24,128]{3,2,1,0:T(8,128)}, u32[]{:S(2)}) %copy-start.1) | copy-done | bytes 1179672
  3.2 0.0 copy-start.2
  3.2 1.0 %copy-done.2 = f32[24,24,128]{2,1,0:T(8,128)S(1)} copy-done((f32[24,24,128]{2,1,0:T(8,128)S(1)}, f32[24,24,128]{2,1,0:T(8,128)}, u32[]{:S(2)}) %copy-start.2) | copy-done | bytes 294936
  4.1 59.7 %shard_map.59 = (f32[2304,128]{1,0:T(8,128)S(1)}, f32[2304,128]{1,0:T(8,128)S(1)}) custom-call(f32[2304,128]{1,0:T(8,128)S(1)} %bitcast.8, f32[2304,128]{1,0:T(8,128)S(1)} %bitcast.9, f32[576,128]{1,0:T(8,128)S(1)} %bitcast.10, f32[3456,128]{1,0:T(8,128)} %bitcast.11), custom_call_target="tpu_custom_call" | custom-call | tf_op jit(solution)/shard_map/pallas_call | solution.py:426
  63.8 1.0 %copy.8 = f32[4,24,24,128]{3,2,1,0:T(8,128)} copy(f32[4,24,24,128]{3,2,1,0:T(8,128)S(1)} %bitcast.7) | data formatting | bytes 2359296
  64.8 1.0 %copy.9 = f32[4,24,24,128]{3,2,1,0:T(8,128)} copy(f32[4,24,24,128]{3,2,1,0:T(8,128)S(1)} %bitcast.6) | data formatting | bytes 2359296
Async XLA Ops:
  0.6 1.3 %copy-start = (f32[4,24,24,128]{3,2,1,0:T(8,128)S(1)}, f32[4,24,24,128]{3,2,1,0:T(8,128)}, u32[]{:S(2)}) copy-start(f32[4,24,24,128]{3,2,1,0:T(8,128)} %param.4) | copy-start | bytes 3538948
  1.9 1.3 %copy-start.1 = (f32[4,24,24,128]{3,2,1,0:T(8,128)S(1)}, f32[4,24,24,128]{3,2,1,0:T(8,128)}, u32[]{:S(2)}) copy-start(f32[4,24,24,128]{3,2,1,0:T(8,128)} %param.5) | copy-start | bytes 3538948
  3.2 1.0 %copy-start.2 = (f32[24,24,128]{2,1,0:T(8,128)S(1)}, f32[24,24,128]{2,1,0:T(8,128)}, u32[]{:S(2)}) copy-start(f32[24,24,128]{2,1,0:T(8,128)} %param.6) | copy-start | bytes 884740
where the time goes:
time: 66.1 us; the launch traced here: 65.8 us
  Pallas kernels  59.7 us (90%)
  local copies, waits for them, and re-layouts  5.52 us (8%)
    pallas_call x1, Pallas kernels, on_device(): pl.pallas_call(functools.partial(kernel, gx_size, gy_size, inner), out_sh...  59.7 us
    unnamed x8, local copies, waits for them, and re-layouts  5.52 us

commit v1 on v0

v1 whole, which is shorter than its diff:
```python
import functools

import jax
import jax.numpy as jnp
from jax import lax
from jax.experimental import pallas as pl
from jax.experimental.pallas import tpu as pltpu
from jax.sharding import PartitionSpec as P

SHIFTS = (12.0, 2.0, 8.0, 5.0)
SCALE_DOWN = 5.0
MESH = pl.DeviceIdType.MESH

R, NZ, BX, L = 4, 24, 24, 128
XT = BX // 8
FR = R * NZ * BX
WR = NZ * BX
PAD = 24
FS = FR + 2 * PAD
HALF = NZ // 2
GROUP = 4
STEPS = NZ // GROUP


def pair_table():
    table, groups, at = {}, [], 0
    for level in range(4):
        for other in (level, 4) + tuple(range(level)):
            pairs = [
                (a, b)
                for a in range(R)
                for b in range(R)
                if other != level or b <= a
            ]
            for index, (a, b) in enumerate(pairs):
                table[(level, a, other, b)] = at + index
            groups.append((level, other, at, pairs))
            at += (len(pairs) + 7) // 8 * 8
    return table, groups, at


TABLE, GROUPS, USED = pair_table()
LANES = 256


def kernel(
    gx_size, gy_size, inner,
    b_hbm, x0_hbm, c_hbm, w_hbm,
    F, W, CS,
    B, C6, WM, WE, WX, HX, HY, XS, YS, HC, RING, RED, RA, RB,
    ld, sx, rx, sy, ry, sa, ra, sb, rb,
):
    gx = lax.axis_index("gx")
    gy = lax.axis_index("gy")
    outer = gx_size // inner
    base_x = (gx // inner) * inner
    in_x = gx - base_x

    loads = [[], [], [], []]
    for group, (source, ref, offset, parts) in enumerate((
        (x0_hbm, F, PAD, R), (w_hbm, WM, 0, 6), (c_hbm, C6, 0, 1), (b_hbm, B, 0, R),
    )):
        rows = source.shape[0] // parts
        for part in range(parts):
            copy = pltpu.make_async_copy(
                source.at[pl.ds(part * rows, rows)],
                ref.at[pl.ds(offset + part * rows, rows)],
                ld.at[group, part],
            )
            copy.start()
            loads[group].append(copy)

    barrier = pltpu.get_barrier_semaphore()
    hello = []
    for step in (1, gx_size - 1):
        hello.append((lax.rem(gx + step, gx_size), gy))
    for step in (1, gy_size - 1):
        hello.append((gx, lax.rem(gy + step, gy_size)))
    inner_peers = [(base_x + lax.rem(in_x + i, inner), gy) for i in range(1, inner)]
    outer_peers = []
    for i in range(outer):
        for j in range(gy_size):
            if i or j:
                outer_peers.append(
                    (lax.rem(gx + i * inner, gx_size), lax.rem(gy + j, gy_size))
                )
    for peer in hello + inner_peers + outer_peers:
        pl.semaphore_signal(barrier, inc=1, device_id=peer, device_id_type=MESH)

    zero = jnp.zeros((8, L), jnp.float32)
    lane = lax.broadcasted_iota(jnp.int32, (8, L), 1)
    sub = lax.broadcasted_iota(jnp.int32, (8, L), 0)
    first_x, last_x = gx == 0, gx == gx_size - 1
    first_y, last_y = gy == 0, gy == gy_size - 1
    for f in range(5):
        for p in range(3):
            F[pl.ds(f * FS + 8 * p, 8), :] = zero
            F[pl.ds(f * FS + PAD + FR + 8 * p, 8), :] = zero

    for cond, ref, side in (
        (first_x, HX, 0), (last_x, HX, 1), (first_y, HY, 0), (last_y, HY, 1),
    ):
        @pl.when(cond)
        def _(ref=ref, side=side):
            for level in range(5):
                for half in range(2):
                    for q in range(ref.shape[3] // 8):
                        ref[level, half, side, pl.ds(8 * q, 8), :] = zero

    tiles = [(xt, r) for xt in range(XT) for r in range(R)]

    def tile_row(r, z, xt):
        return (r * NZ + z) * BX + 8 * xt

    def aligned(row):
        return row if isinstance(row, int) else pl.multiple_of(row, 8)

    def pack_lane(r, zh):
        return 2 * (r * HALF + zh)

    def pack_tile(tile, r, zh, acc):
        j2 = pack_lane(r, zh)
        mask = ((lane + (1 - j2)) & (L - 1)) < 2
        return jnp.where(mask, pltpu.roll(tile, j2, 1), acc)

    def copies(level, half):
        result = []
        for missing, lands, takes, gap, row in (
            (last_x, 0, 1, (gx + 1, gy), XS), (first_x, 1, 0, (gx - 1, gy), XS),
            (last_y, 0, None, (gx, gy + 1), YS), (first_y, 1, None, (gx, gy - 1), YS),
        ):
            along_x = row is XS
            source = XS.at[level, half, takes] if along_x else YS.at[level, half]
            target = (HX if along_x else HY).at[level, half, lands]
            out_sem, in_sem = (sx, rx) if along_x else (sy, ry)
            result.append((missing, pltpu.make_async_remote_copy(
                src_ref=source, dst_ref=target,
                send_sem=out_sem.at[level, half, lands], recv_sem=in_sem.at[level, half, lands],
                device_id=gap, device_id_type=MESH)))
        return result

    def send(level, half, acc):
        for xt in range(XT):
            YS[level, half, pl.ds(8 * xt, 8), :] = acc[xt]
        for missing, copy in copies(level, half):
            @pl.when(jnp.logical_not(missing))
            def _(copy=copy):
                copy.start()

    def receive(level, half):
        for missing, (_, copy) in zip(
            (first_x, last_x, first_y, last_y), copies(level, half)
        ):
            @pl.when(jnp.logical_not(missing))
            def _(copy=copy):
                copy.wait_recv()

    def sent(level):
        for half in range(2):
            for missing, copy in copies(level, half):
                @pl.when(jnp.logical_not(missing))
                def _(copy=copy):
                    copy.wait_send()

    def bulk(level):
        base = level * FS + PAD
        out = max(level - 1, 0) * FR
        slot = 2 * GROUP * R * XT * 8

        def keep_rolls(z0, at):
            kept = []
            for k in range(GROUP):
                for index, (xt, r) in enumerate(tiles):
                    mid = F[pl.ds(aligned(base + tile_row(r, z0 + k, xt)), 8), :]
                    where = at + 16 * (k * R * XT + index)
                    kept.append((where, pltpu.roll(mid, 1, 1)))
                    kept.append((where + 8, pltpu.roll(mid, L - 1, 1)))
            return kept

        for at, value in keep_rolls(0, 0):
            RING[pl.ds(at, 8), :] = value

        def body(step, carry):
            now = pl.multiple_of(lax.rem(step, 2) * slot, 8)
            later = pl.multiple_of(slot - now, 8)
            kept = keep_rolls(jnp.minimum(step + 1, STEPS - 1) * GROUP, later)
            stores = []
            for k in range(GROUP):
                z = step * GROUP + k
                for xt in range(XT):
                    wrow = pl.multiple_of(z * BX + 8 * xt, 8)
                    w = [WM[pl.ds(i * WR + wrow, 8), :] for i in range(6)]
                    c6 = C6[pl.ds(wrow, 8), :]
                    for r in range(R):
                        ring = now + 16 * ((k * XT + xt) * R + r)
                        row = pl.multiple_of(tile_row(r, z, xt), 8)
                        at = base + row
                        low = RING[pl.ds(ring, 8), :]
                        high = RING[pl.ds(ring + 8, 8), :]
                        beside = w[0] * F[pl.ds(at - 1, 8), :] + w[1] * F[pl.ds(at + 1, 8), :]
                        beside = beside + (w[2] * low + w[3] * high)
                        beside = beside + (
                            w[4] * F[pl.ds(at - BX, 8), :] + w[5] * F[pl.ds(at + BX, 8), :]
                        )
                        stores.append((out + row, c6 * F[pl.ds(at, 8), :] - beside))
            for at, value in stores:
                W[pl.ds(at, 8), :] = value
            for at, value in kept:
                RING[pl.ds(at, 8), :] = value
            return carry

        lax.fori_loop(0, STEPS, body, 0)

    def correct(level, half):
        out = max(level - 1, 0) * FR
        even = (lane & 1) == 0
        for xt in range(XT):
            HC[pl.ds(8 * xt, 8), :] = jnp.where(
                even,
                pltpu.roll(HY[level, half, 0, pl.ds(8 * xt, 8), :], 1, 1),
                pltpu.roll(HY[level, half, 1, pl.ds(8 * xt, 8), :], L - 1, 1),
            )
        slot = GROUP * R * XT * 8
        ahead = (level + 1) * FS + PAD
        steps = HALF // GROUP

        def keep_halos(step, at):
            kept = []
            for k in range(GROUP):
                for index, (xt, r) in enumerate(tiles):
                    back = lax.rem(2 * L - pack_lane(r, step * GROUP + k), L)
                    halo = pltpu.roll(HC[pl.ds(8 * xt, 8), :], back, 1)
                    kept.append((at + 8 * (k * R * XT + index), halo))
            return kept

        def pack_planes(step, acc):
            for k in range(GROUP):
                zh = step * GROUP + k
                for xt, r in tiles:
                    row = aligned(tile_row(r, half * HALF + zh, xt))
                    acc[xt] = pack_tile(F[pl.ds(ahead + row, 8), :], r, zh, acc[xt])

        for at, value in keep_halos(0, 0):
            RING[pl.ds(at, 8), :] = value

        def body(step, acc):
            acc = list(acc)
            now = pl.multiple_of(lax.rem(step, 2) * slot, 8)
            later = pl.multiple_of(slot - now, 8)
            kept = keep_halos(jnp.minimum(step + 1, steps - 1), later)
            if level < 4:
                pack_planes(jnp.maximum(step - 1, 0), acc)
            stores, nexts, rows = [], [], []
            for k in range(GROUP):
                zh = step * GROUP + k
                z = half * HALF + zh
                for xt in range(XT):
                    edge = WE[pl.ds(pl.multiple_of(z * BX + 8 * xt, 8), 8), :]
                    for r in range(R):
                        row = pl.multiple_of(tile_row(r, z, xt), 8)
                        halo = RING[pl.ds(now + 8 * ((k * XT + xt) * R + r), 8), :]
                        image = W[pl.ds(out + row, 8), :] - edge * halo
                        for side, where in ((0, 0), (1, XT - 1)):
                            if xt == where:
                                edge_x = WX[pl.ds(pl.multiple_of((side * NZ + z) * 8, 8), 8), :]
                                halo_x = HX[level, half, side, pl.ds(r * HALF + zh, 1), :]
                                image = image - edge_x * jnp.broadcast_to(halo_x, (8, L))
                        if level == 0:
                            following = B[pl.ds(row, 8), :] - image
                        else:
                            stores.append((out + row, image))
                            held = F[pl.ds(level * FS + PAD + row, 8), :]
                            following = image * (1.0 / SCALE_DOWN) - held * (
                                SHIFTS[level - 1] / SCALE_DOWN
                            )
                        if level < 4:
                            nexts.append((ahead + row, following))
                            for side, where, take in ((0, 0, 0), (1, XT - 1, 7)):
                                if xt == where:
                                    rows.append((side, r * HALF + zh, following[take : take + 1]))
            for at, value in stores:
                W[pl.ds(at, 8), :] = value
            for at, value in nexts:
                F[pl.ds(at, 8), :] = value
            for side, at, value in rows:
                XS[level + 1, half, side, pl.ds(at, 1), :] = value
            for at, value in kept:
                RING[pl.ds(at, 8), :] = value
            return tuple(acc)

        acc = list(lax.fori_loop(0, steps, body, (zero,) * XT))
        if level < 4:
            pack_planes(steps - 1, acc)
        return acc

    def combine(a, b, d):
        mask = (sub & d) == 0
        return jnp.where(mask, a, b) + pltpu.roll(jnp.where(mask, b, a), d, 0)

    def gram(level):
        for lev, other, start, pairs in GROUPS:
            if lev != level:
                continue

            def rows_of(block, r, z, xt):
                row = pl.multiple_of(tile_row(r, z, xt), 8)
                if block == 4:
                    return F[pl.ds(FS + PAD + row, 8), :]
                return W[pl.ds(block * FR + row, 8), :]

            def body(step, acc):
                acc = list(acc)
                for z, xt in [(2 * step + k, xt) for k in range(2) for xt in range(XT)]:
                    left = [rows_of(lev, r, z, xt) for r in range(R)]
                    right = left
                    if other != lev:
                        right = [rows_of(other, r, z, xt) for r in range(R)]
                    for index, (a, b) in enumerate(pairs):
                        acc[index] = acc[index] + left[a] * right[b]
                return tuple(acc)

            sums = list(lax.fori_loop(0, NZ // 2, body, (zero,) * len(pairs)))
            sums += [zero] * (-len(sums) % 8)
            for q in range(0, len(sums), 8):
                part = sums[q : q + 8]
                for d in (1, 2, 4):
                    part = [combine(part[k], part[k + 1], d) for k in range(0, len(part), 2)]
                RED[pl.ds(start + q, 8), :] = part[0]

    for copy in loads[0]:
        copy.wait()

    packed = []
    for half in range(2):
        def pack_body(step, acc, half=half):
            acc = list(acc)
            for k in range(GROUP):
                zh = step * GROUP + k
                for xt, r in tiles:
                    row = pl.multiple_of(PAD + tile_row(r, half * HALF + zh, xt), 8)
                    tile = F[pl.ds(row, 8), :]
                    acc[xt] = pack_tile(tile, r, zh, acc[xt])
                    for side, where, take in ((0, 0, 0), (1, XT - 1, 7)):
                        if xt == where:
                            XS[0, half, side, pl.ds(r * HALF + zh, 1), :] = tile[take : take + 1]
            return tuple(acc)

        packed.append(lax.fori_loop(0, HALF // GROUP, pack_body, (zero,) * XT))
    pl.semaphore_wait(barrier, len(hello) + len(inner_peers) + len(outer_peers))
    for half in range(2):
        send(0, half, packed[half])

    for copy in loads[1] + loads[2]:
        copy.wait()

    def prepare(z, carry):
        stores = []
        for xt in range(XT):
            row = pl.multiple_of(z * BX + 8 * xt, 8)
            stores.append((C6, row, C6[pl.ds(row, 8), :] + 6.0))
            for side, where, inside in ((0, 0, sub != 0), (1, XT - 1, sub != 7)):
                if xt == where:
                    w = WM[pl.ds(side * WR + row, 8), :]
                    stores.append((WM, side * WR + row, jnp.where(inside, w, 0.0)))
                    at = pl.multiple_of((side * NZ + z) * 8, 8)
                    stores.append((WX, at, jnp.where(inside, 0.0, w)))
            low = WM[pl.ds(2 * WR + row, 8), :]
            high = WM[pl.ds(3 * WR + row, 8), :]
            edge = jnp.where(lane == 0, low, jnp.where(lane == L - 1, high, 0.0))
            stores.append((WE, row, edge))
            stores.append((WM, 2 * WR + row, jnp.where(lane == 0, 0.0, low)))
            stores.append((WM, 3 * WR + row, jnp.where(lane == L - 1, 0.0, high)))
        for ref, at, value in stores:
            ref[pl.ds(at, 8), :] = value
        return carry

    lax.fori_loop(0, NZ, prepare, 0)
    for xt in range(XT):
        WM[pl.ds(4 * WR + 8 * xt, 8), :] = zero
        WM[pl.ds(5 * WR + (NZ - 1) * BX + 8 * xt, 8), :] = zero
    bulk(0)
    for copy in loads[3]:
        copy.wait()
    for level in range(5):
        for half in range(2):
            receive(level, half)
            acc = correct(level, half)
            if level < 4:
                send(level + 1, half, acc)
        if level < 4:
            bulk(level + 1)
            if level >= 1:
                gram(level - 1)
        sent(level)
    gram(3)

    for q in range(USED, LANES, 8):
        RED[pl.ds(q, 8), :] = zero
    total = lax.dot_general(
        jnp.ones((8, L), jnp.float32), RED[...], (((1,), (1,)), ((), ())),
        precision=lax.Precision.HIGHEST, preferred_element_type=jnp.float32,
    )

    def exchange(total, buffer, peers, send_sems, recv_sems):
        buffer[0] = total
        copies = []
        for k, peer in enumerate(peers):
            copy = pltpu.make_async_remote_copy(
                src_ref=buffer.at[0], dst_ref=buffer.at[k + 1],
                send_sem=send_sems.at[k], recv_sem=recv_sems.at[k],
                device_id=peer, device_id_type=MESH,
            )
            copy.start()
            copies.append(copy)
        for copy in copies:
            copy.wait_recv()
        parts = [buffer[k] for k in range(len(peers) + 1)]
        while len(parts) > 1:
            parts = [
                parts[k] + parts[k + 1] if k + 1 < len(parts) else parts[k]
                for k in range(0, len(parts), 2)
            ]
        for copy in copies:
            copy.wait_send()
        return parts[0]

    total = exchange(total, RA, inner_peers, sa, ra)
    total = exchange(total, RB, outer_peers, sb, rb)

    def entry(p):
        block = total[:, (p // L) * L : (p // L + 1) * L]
        return jnp.broadcast_to(block[:, p % L : p % L + 1], (8, L))

    order = 16
    A = {}
    for i in range(order):
        for j in range(i + 1):
            A[i, j] = entry(TABLE[(i // R, i % R, j // R, j % R)])
    rhs = []
    for i in range(order):
        column = [entry(TABLE[(i // R, i % R, 4, r)]) for r in range(R)]
        rhs.append(
            jnp.where(sub == 0, column[0],
                      jnp.where(sub == 1, column[1],
                                jnp.where(sub == 2, column[2], column[3])))
        )
    lower, inverse = {}, []
    for k in range(order):
        inv = 1.0 / A[k, k]
        inverse.append(inv)
        for i in range(k + 1, order):
            lower[i, k] = A[i, k] * inv
        for i in range(k + 1, order):
            for j in range(k + 1, i + 1):
                A[i, j] = A[i, j] - lower[i, k] * A[j, k]
            rhs[i] = rhs[i] - lower[i, k] * rhs[k]
    coeffs = [None] * order
    for k in range(order - 1, -1, -1):
        value = rhs[k] * inverse[k]
        for i in range(order - 1, k, -1):
            value = value - lower[i, k] * coeffs[i]
        coeffs[k] = value
        for r in range(R):
            CS[pl.ds((r * order + k) * 8, 8), :] = jnp.broadcast_to(value[r : r + 1], (8, L))


def update(F, W, CS, x0, sol, res):
    step = pl.program_id(0)
    planes = NZ // UPDATE_STEPS

    def body(k, carry):
        z = step * planes + k
        stores = []
        for r in range(R):
            for xt in range(XT):
                row = pl.multiple_of((r * NZ + z) * BX + 8 * xt, 8)
                stores.append([x0[r, k, pl.ds(8 * xt, 8), :], F[pl.ds(FS + PAD + row, 8), :]])
        for i in range(16):
            coef = [CS[pl.ds((r * 16 + i) * 8, 8), :] for r in range(R)]
            for xt in range(XT):
                row = pl.multiple_of(((i % R) * NZ + z) * BX + 8 * xt, 8)
                basis = F[pl.ds((i // R + 1) * FS + PAD + row, 8), :]
                image = W[pl.ds((i // R) * FR + row, 8), :]
                for r in range(R):
                    both = stores[r * XT + xt]
                    both[0] = both[0] + coef[r] * basis
                    both[1] = both[1] - coef[r] * image
        for r in range(R):
            for xt in range(XT):
                sol[r, k, pl.ds(8 * xt, 8), :] = stores[r * XT + xt][0]
                res[r, k, pl.ds(8 * xt, 8), :] = stores[r * XT + xt][1]
        return carry

    lax.fori_loop(0, planes, body, 0)


UPDATE_STEPS = 4


def on_device(gx_size, gy_size, right_side, start_field, center, weights):
    inner = min(8, gx_size // 2)
    outer = gx_size // inner
    dma = pltpu.SemaphoreType.DMA
    f32 = jnp.float32
    flat = lambda a: a.reshape(-1, L)
    held = pltpu.MemorySpace.VMEM
    shape = lambda *dims: jax.ShapeDtypeStruct(dims, f32)
    in_hbm = lambda a: pltpu.with_memory_space_constraint(flat(a), pltpu.HBM)
    fields, images, coeffs = pl.pallas_call(
        functools.partial(kernel, gx_size, gy_size, inner),
        out_shape=[shape(5 * FS, L), shape(4 * FR, L), shape(64 * 8, L)],
        in_specs=[pl.BlockSpec(memory_space=pltpu.HBM)] * 4,
        out_specs=[pl.BlockSpec(memory_space=held)] * 3,
        scratch_shapes=[
            pltpu.VMEM((FR, L), f32),
            pltpu.VMEM((WR, L), f32),
            pltpu.VMEM((6 * WR, L), f32),
            pltpu.VMEM((WR, L), f32),
            pltpu.VMEM((2 * NZ * 8, L), f32),
            pltpu.VMEM((5, 2, 2, R * HALF, L), f32),
            pltpu.VMEM((5, 2, 2, BX, L), f32),
            pltpu.VMEM((5, 2, 2, R * HALF, L), f32),
            pltpu.VMEM((5, 2, BX, L), f32),
            pltpu.VMEM((BX, L), f32),
            pltpu.VMEM((2 * 2 * GROUP * R * XT * 8, L), f32),
            pltpu.VMEM((LANES, L), f32),
            pltpu.VMEM((inner, 8, LANES), f32),
            pltpu.VMEM((outer * gy_size, 8, LANES), f32),
            dma((4, 6)),
            dma((5, 2, 2)), dma((5, 2, 2)), dma((5, 2, 2)), dma((5, 2, 2)),
            dma((inner,)), dma((inner,)),
            dma((outer * gy_size,)), dma((outer * gy_size,)),
        ],
        compiler_params=pltpu.CompilerParams(
            collective_id=0, has_side_effects=True, vmem_limit_bytes=32 * 1024 * 1024,
        ),
    )(in_hbm(right_side), in_hbm(start_field), in_hbm(center), in_hbm(weights))
    block = pl.BlockSpec((R, NZ // UPDATE_STEPS, BX, L), lambda i: (0, i, 0, 0))
    return pl.pallas_call(
        update,
        grid=(UPDATE_STEPS,),
        out_shape=[shape(R, NZ, BX, L)] * 2,
        in_specs=[pl.BlockSpec(memory_space=held)] * 3 + [block],
        out_specs=[block, block],
        compiler_params=pltpu.CompilerParams(vmem_limit_bytes=24 * 1024 * 1024),
    )(fields, images, coeffs, pltpu.with_memory_space_constraint(start_field, pltpu.HBM))


def solution(mesh):
    gx_size, gy_size = mesh.shape["gx"], mesh.shape["gy"]
    return jax.shard_map(
        functools.partial(on_device, gx_size, gy_size),
        mesh=mesh,
        in_specs=(
            P(None, None, "gx", "gy"),
            P(None, None, "gx", "gy"),
            P(None, "gx", "gy"),
            P(None, None, "gx", "gy"),
        ),
        out_specs=(P(None, None, "gx", "gy"), P(None, None, "gx", "gy")),
        check_vma=False,
    )
```

time: 66.1 us -> 48.3 us (0.73)
  Pallas kernels: 59.7 us -> 47.5 us
  local copies, waits for them, and re-layouts: 5.52 us -> 0 us
    pallas_call x1, Pallas kernels: 59.7 us -> 42.1 us  [on_device(): pl.pallas_call(functools.partial(kernel, gx_size, gy_size, inner), out_sh...]
    unnamed x8 -> x0, local copies, waits for them, and re-layouts: 5.52 us -> none
    pallas_call x0 -> x1, Pallas kernels: none -> 5.36 us  [on_device(): pl.pallas_call(update, grid=(UPDATE_STEPS,), out_shape=[shape(R, NZ, BX,...]
where the time goes in v1:
time: 48.3 us; the launch traced here: 48.1 us
  Pallas kernels  47.5 us (98%)
  between operations  0.64 us (1%)
    pallas_call x1, Pallas kernels, on_device(): pl.pallas_call(functools.partial(kernel, gx_size, gy_size, inner), out_sh...  42.1 us
    pallas_call x1, Pallas kernels, on_device(): pl.pallas_call(update, grid=(UPDATE_STEPS,), out_shape=[shape(R, NZ, BX,...  5.36 us

profile of v1, /device:TPU:1, one launch (start us, length us, event | category | flops | bytes accessed | tf_op | source)
XLA Modules:
  0.0 48.1 jit_solution(5760862931904548724)
XLA Ops:
  0.6 42.1 %shard_map.59 = (f32[11760,128]{1,0:T(8,128)S(1)}, f32[9216,128]{1,0:T(8,128)S(1)}, f32[512,128]{1,0:T(8,128)S(1)}) custom-call(f32[2304,128]{1,0:T(8,128)} %bitcast.6, f32[2304,128]{1,0:T(8,128)} %bitcast.4, f32[576,128]{1,0:T(8,128)} %bitcast.7, f32[3456,128]{1,0:T(8,128)} %bitcast.5), custom_call_target="tpu_custom_call" | custom-call | tf_op jit(solution)/shard_map/pallas_call | solution.py:509
  42.8 5.4 %shard_map.60 = (f32[4,24,24,128]{3,2,1,0:T(8,128)}, f32[4,24,24,128]{3,2,1,0:T(8,128)}) custom-call(f32[11760,128]{1,0:T(8,128)S(1)} %get-tuple-element.5.F, f32[9216,128]{1,0:T(8,128)S(1)} %get-tuple-element.6.W, f32[512,128]{1,0:T(8,128)S(1)} %get-tuple-element.7.CS, f32[4,24,24,128]{3,2,1,0:T(8,128)} %x0.1), custom_call_target="tpu_custom_call" | custom-call | tf_op jit(solution)/shard_map/pallas_call | solution.py:539

commit v2 on v1

--- a/solution.py
+++ b/solution.py
@@ -47,7 +47,7 @@
     gx_size, gy_size, inner,
     b_hbm, x0_hbm, c_hbm, w_hbm,
     F, W, CS,
-    B, C6, WM, WE, WX, HX, HY, XS, YS, HC, RING, RED, RA, RB,
+    B, C6, WM, WE, WX, HX, HY, XS, YS, RING, ACC, RED, RA, RB,
     ld, sx, rx, sy, ry, sa, ra, sb, rb,
 ):
     gx = lax.axis_index("gx")
@@ -67,8 +67,9 @@
                 ref.at[pl.ds(offset + part * rows, rows)],
                 ld.at[group, part],
             )
-            copy.start()
             loads[group].append(copy)
+    for copy in loads[0] + loads[2] + loads[1]:
+        copy.start()
 
     barrier = pltpu.get_barrier_semaphore()
     hello = []
@@ -162,12 +163,10 @@
                 def _(copy=copy):
                     copy.wait_send()
 
-    def bulk(level):
-        base = level * FS + PAD
-        out = max(level - 1, 0) * FR
-        slot = 2 * GROUP * R * XT * 8
-
-        def keep_rolls(z0, at):
+    slot = 2 * GROUP * R * XT * 8
+
+    def keep_rolls(level, z0, at):
+            base = level * FS + PAD
             kept = []
             for k in range(GROUP):
                 for index, (xt, r) in enumerate(tiles):
@@ -177,13 +176,43 @@
                     kept.append((where + 8, pltpu.roll(mid, L - 1, 1)))
             return kept
 
-        for at, value in keep_rolls(0, 0):
+    def first_rolls(level):
+        for at, value in keep_rolls(level, 0, 0):
             RING[pl.ds(at, 8), :] = value
+
+    def rows_of(block, r, z, xt):
+        row = aligned(tile_row(r, z, xt))
+        if block == 4:
+            return F[pl.ds(FS + PAD + row, 8), :]
+        return W[pl.ds(block * FR + row, 8), :]
+
+    def products(lev, other, pairs, places, acc):
+        for z, xt in places:
+            left = [rows_of(lev, r, z, xt) for r in range(R)]
+            right = left if other == lev else [rows_of(other, r, z, xt) for r in range(R)]
+            for index, (a, b) in enumerate(pairs):
+                acc[index] = acc[index] + left[a] * right[b]
+
+    def fold(sums, start):
+        sums = sums + [zero] * (-len(sums) % 8)
+        for q in range(0, len(sums), 8):
+            part = sums[q : q + 8]
+            for d in (1, 2, 4):
+                part = [combine(part[k], part[k + 1], d) for k in range(0, len(part), 2)]
+            RED[pl.ds(start + q, 8), :] = part[0]
+
+    def bulk(level, gram_level=None):
+        base = level * FS + PAD
+        out = max(level - 1, 0) * FR
+        groups = [g for g in GROUPS if g[0] == gram_level]
+        for _, _, start, pairs in groups:
+            for index in range(len(pairs)):
+                ACC[pl.ds(8 * (start + index), 8), :] = zero
 
         def body(step, carry):
             now = pl.multiple_of(lax.rem(step, 2) * slot, 8)
             later = pl.multiple_of(slot - now, 8)
-            kept = keep_rolls(jnp.minimum(step + 1, STEPS - 1) * GROUP, later)
+            kept = keep_rolls(level, jnp.minimum(step + 1, STEPS - 1) * GROUP, later)
             stores = []
             for k in range(GROUP):
                 z = step * GROUP + k
@@ -203,6 +232,13 @@
                             w[4] * F[pl.ds(at - BX, 8), :] + w[5] * F[pl.ds(at + BX, 8), :]
                         )
                         stores.append((out + row, c6 * F[pl.ds(at, 8), :] - beside))
+            places = [(step * GROUP + k, xt) for k in range(GROUP) for xt in range(XT)]
+            for lev, other, start, pairs in groups:
+                where = [pl.ds(8 * (start + index), 8) for index in range(len(pairs))]
+                acc = [ACC[w, :] for w in where]
+                products(lev, other, pairs, places, acc)
+                for w, value in zip(where, acc):
+                    ACC[w, :] = value
             for at, value in stores:
                 W[pl.ds(at, 8), :] = value
             for at, value in kept:
@@ -210,87 +246,51 @@
             return carry
 
         lax.fori_loop(0, STEPS, body, 0)
+        for _, _, start, pairs in groups:
+            fold([ACC[pl.ds(8 * (start + index), 8), :] for index in range(len(pairs))], start)
 
     def correct(level, half):
         out = max(level - 1, 0) * FR
+        ahead = (level + 1) * FS + PAD
         even = (lane & 1) == 0
-        for xt in range(XT):
-            HC[pl.ds(8 * xt, 8), :] = jnp.where(
+        halos = [
+            jnp.where(
                 even,
                 pltpu.roll(HY[level, half, 0, pl.ds(8 * xt, 8), :], 1, 1),
                 pltpu.roll(HY[level, half, 1, pl.ds(8 * xt, 8), :], L - 1, 1),
             )
-        slot = GROUP * R * XT * 8
-        ahead = (level + 1) * FS + PAD
-        steps = HALF // GROUP
-
-        def keep_halos(step, at):
-            kept = []
-            for k in range(GROUP):
-                for index, (xt, r) in enumerate(tiles):
-                    back = lax.rem(2 * L - pack_lane(r, step * GROUP + k), L)
-                    halo = pltpu.roll(HC[pl.ds(8 * xt, 8), :], back, 1)
-                    kept.append((at + 8 * (k * R * XT + index), halo))
-            return kept
-
-        def pack_planes(step, acc):
-            for k in range(GROUP):
-                zh = step * GROUP + k
-                for xt, r in tiles:
-                    row = aligned(tile_row(r, half * HALF + zh, xt))
-                    acc[xt] = pack_tile(F[pl.ds(ahead + row, 8), :], r, zh, acc[xt])
-
-        for at, value in keep_halos(0, 0):
-            RING[pl.ds(at, 8), :] = value
-
-        def body(step, acc):
-            acc = list(acc)
-            now = pl.multiple_of(lax.rem(step, 2) * slot, 8)
-            later = pl.multiple_of(slot - now, 8)
-            kept = keep_halos(jnp.minimum(step + 1, steps - 1), later)
-            if level < 4:
-                pack_planes(jnp.maximum(step - 1, 0), acc)
-            stores, nexts, rows = [], [], []
-            for k in range(GROUP):
-                zh = step * GROUP + k
-                z = half * HALF + zh
-                for xt in range(XT):
-                    edge = WE[pl.ds(pl.multiple_of(z * BX + 8 * xt, 8), 8), :]
-                    for r in range(R):
-                        row = pl.multiple_of(tile_row(r, z, xt), 8)
-                        halo = RING[pl.ds(now + 8 * ((k * XT + xt) * R + r), 8), :]
-                        image = W[pl.ds(out + row, 8), :] - edge * halo
-                        for side, where in ((0, 0), (1, XT - 1)):
-                            if xt == where:
-                                edge_x = WX[pl.ds(pl.multiple_of((side * NZ + z) * 8, 8), 8), :]
-                                halo_x = HX[level, half, side, pl.ds(r * HALF + zh, 1), :]
-                                image = image - edge_x * jnp.broadcast_to(halo_x, (8, L))
-                        if level == 0:
-                            following = B[pl.ds(row, 8), :] - image
-                        else:
-                            stores.append((out + row, image))
-                            held = F[pl.ds(level * FS + PAD + row, 8), :]
-                            following = image * (1.0 / SCALE_DOWN) - held * (
-                                SHIFTS[level - 1] / SCALE_DOWN
+            for xt in range(XT)
+        ]
+        acc = [zero] * XT
+        for zh in range(HALF):
+            z = half * HALF + zh
+            for xt, r in tiles:
+                row = tile_row(r, z, xt)
+                halo = pltpu.roll(halos[xt], (L - pack_lane(r, zh)) % L, 1)
+                image = W[pl.ds(out + row, 8), :] - WE[pl.ds(z * BX + 8 * xt, 8), :] * halo
+                for side, where in ((0, 0), (1, XT - 1)):
+                    if xt == where:
+                        edge_x = WX[pl.ds((side * NZ + z) * 8, 8), :]
+                        halo_x = HX[level, half, side, pl.ds(r * HALF + zh, 1), :]
+                        image = image - edge_x * jnp.broadcast_to(halo_x, (8, L))
+                if level == 0:
+                    following = B[pl.ds(row, 8), :] - image
+                else:
+                    W[pl.ds(out + row, 8), :] = image
+                    held = F[pl.ds(level * FS + PAD + row, 8), :]
+                    following = image * (1.0 / SCALE_DOWN) - held * (
+                        SHIFTS[level - 1] / SCALE_DOWN
+                    )
+                if level < 4:
+                    F[pl.ds(ahead + row, 8), :] = following
+                    for side, where, take in ((0, 0, 0), (1, XT - 1, 7)):
+                        if xt == where:
+                            XS[level + 1, half, side, pl.ds(r * HALF + zh, 1), :] = (
+                                following[take : take + 1]
                             )
-                        if level < 4:
-                            nexts.append((ahead + row, following))
-                            for side, where, take in ((0, 0, 0), (1, XT - 1, 7)):
-                                if xt == where:
-                                    rows.append((side, r * HALF + zh, following[take : take + 1]))
-            for at, value in stores:
-                W[pl.ds(at, 8), :] = value
-            for at, value in nexts:
-                F[pl.ds(at, 8), :] = value
-            for side, at, value in rows:
-                XS[level + 1, half, side, pl.ds(at, 1), :] = value
-            for at, value in kept:
-                RING[pl.ds(at, 8), :] = value
-            return tuple(acc)
-
-        acc = list(lax.fori_loop(0, steps, body, (zero,) * XT))
-        if level < 4:
-            pack_planes(steps - 1, acc)
+                    acc[xt] = pack_tile(following, r, zh, acc[xt])
+        if half and level < 4:
+            first_rolls(level + 1)
         return acc
 
     def combine(a, b, d):
@@ -302,33 +302,18 @@
             if lev != level:
                 continue
 
-            def rows_of(block, r, z, xt):
-                row = pl.multiple_of(tile_row(r, z, xt), 8)
-                if block == 4:
-                    return F[pl.ds(FS + PAD + row, 8), :]
-                return W[pl.ds(block * FR + row, 8), :]
-
             def body(step, acc):
                 acc = list(acc)
-                for z, xt in [(2 * step + k, xt) for k in range(2) for xt in range(XT)]:
-                    left = [rows_of(lev, r, z, xt) for r in range(R)]
-                    right = left
-                    if other != lev:
-                        right = [rows_of(other, r, z, xt) for r in range(R)]
-                    for index, (a, b) in enumerate(pairs):
-                        acc[index] = acc[index] + left[a] * right[b]
+                places = [(2 * step + k, xt) for k in range(2) for xt in range(XT)]
+                products(lev, other, pairs, places, acc)
                 return tuple(acc)
 
-            sums = list(lax.fori_loop(0, NZ // 2, body, (zero,) * len(pairs)))
-            sums += [zero] * (-len(sums) % 8)
-            for q in range(0, len(sums), 8):
-                part = sums[q : q + 8]
-                for d in (1, 2, 4):
-                    part = [combine(part[k], part[k + 1], d) for k in range(0, len(part), 2)]
-                RED[pl.ds(start + q, 8), :] = part[0]
+            fold(list(lax.fori_loop(0, NZ // 2, body, (zero,) * len(pairs))), start)
 
     for copy in loads[0]:
         copy.wait()
+    for copy in loads[3]:
+        copy.start()
 
     packed = []
     for half in range(2):
@@ -378,6 +363,7 @@
     for xt in range(XT):
         WM[pl.ds(4 * WR + 8 * xt, 8), :] = zero
         WM[pl.ds(5 * WR + (NZ - 1) * BX + 8 * xt, 8), :] = zero
+    first_rolls(0)
     bulk(0)
     for copy in loads[3]:
         copy.wait()
@@ -388,9 +374,7 @@
             if level < 4:
                 send(level + 1, half, acc)
         if level < 4:
-            bulk(level + 1)
-            if level >= 1:
-                gram(level - 1)
+            bulk(level + 1, level - 1)
         sent(level)
     gram(3)
 
@@ -402,19 +386,24 @@
     )
 
     def exchange(total, buffer, peers, send_sems, recv_sems):
-        buffer[0] = total
+        buffer[pl.ds(0, 8), :] = total
         copies = []
         for k, peer in enumerate(peers):
             copy = pltpu.make_async_remote_copy(
-                src_ref=buffer.at[0], dst_ref=buffer.at[k + 1],
+                src_ref=buffer.at[pl.ds(0, 2)], dst_ref=buffer.at[pl.ds(8 + 2 * k, 2)],
                 send_sem=send_sems.at[k], recv_sem=recv_sems.at[k],
                 device_id=peer, device_id_type=MESH,
             )
             copy.start()
             copies.append(copy)
+        own = jnp.where(sub < 2, total, 0.0)
         for copy in copies:
             copy.wait_recv()
-        parts = [buffer[k] for k in range(len(peers) + 1)]
+        parts = [own]
+        for at in range(0, 2 * len(peers), 8):
+            part = buffer[pl.ds(8 + at, 8), :]
+            left = 2 * len(peers) - at
+            parts.append(part if left >= 8 else jnp.where(sub < left, part, 0.0))
         while len(parts) > 1:
             parts = [
                 parts[k] + parts[k + 1] if k + 1 < len(parts) else parts[k]
@@ -422,14 +411,20 @@
             ]
         for copy in copies:
             copy.wait_send()
-        return parts[0]
-
+        total = parts[0]
+        for d in (2, 4):
+            total = total + pltpu.roll(total, d, 0)
+        return total
+
+    total = jnp.where((sub & 1) == 0, total[:, :L], total[:, L:])
     total = exchange(total, RA, inner_peers, sa, ra)
     total = exchange(total, RB, outer_peers, sb, rb)
+    swapped = pltpu.roll(total, 1, 0)
+    even_row = (sub & 1) == 0
+    total = [jnp.where(even_row, total, swapped), jnp.where(even_row, swapped, total)]
 
     def entry(p):
-        block = total[:, (p // L) * L : (p // L + 1) * L]
-        return jnp.broadcast_to(block[:, p % L : p % L + 1], (8, L))
+        return jnp.broadcast_to(total[p // L][:, p % L : p % L + 1], (8, L))
 
     order = 16
     A = {}
@@ -464,37 +459,52 @@
             CS[pl.ds((r * order + k) * 8, 8), :] = jnp.broadcast_to(value[r : r + 1], (8, L))
 
 
-def update(F, W, CS, x0, sol, res):
-    step = pl.program_id(0)
+UPDATE_STEPS = 8
+
+
+def update(F, W, CS, sol_hbm, res_hbm, sol, res, sems):
     planes = NZ // UPDATE_STEPS
 
-    def body(k, carry):
-        z = step * planes + k
-        stores = []
-        for r in range(R):
-            for xt in range(XT):
-                row = pl.multiple_of((r * NZ + z) * BX + 8 * xt, 8)
-                stores.append([x0[r, k, pl.ds(8 * xt, 8), :], F[pl.ds(FS + PAD + row, 8), :]])
-        for i in range(16):
-            coef = [CS[pl.ds((r * 16 + i) * 8, 8), :] for r in range(R)]
-            for xt in range(XT):
-                row = pl.multiple_of(((i % R) * NZ + z) * BX + 8 * xt, 8)
-                basis = F[pl.ds((i // R + 1) * FS + PAD + row, 8), :]
-                image = W[pl.ds((i // R) * FR + row, 8), :]
-                for r in range(R):
-                    both = stores[r * XT + xt]
-                    both[0] = both[0] + coef[r] * basis
-                    both[1] = both[1] - coef[r] * image
-        for r in range(R):
-            for xt in range(XT):
-                sol[r, k, pl.ds(8 * xt, 8), :] = stores[r * XT + xt][0]
-                res[r, k, pl.ds(8 * xt, 8), :] = stores[r * XT + xt][1]
+    def writes(step):
+        where = (slice(None), pl.ds(step * planes, planes))
+        return [
+            pltpu.make_async_copy(source.at[where], target.at[where], sems.at[k, step])
+            for k, (source, target) in enumerate(((sol, sol_hbm), (res, res_hbm)))
+        ]
+
+    def body(step, carry):
+        def plane(k, carry):
+            z = step * planes + k
+            sums = []
+            for r in range(R):
+                for xt in range(XT):
+                    row = pl.multiple_of((r * NZ + z) * BX + 8 * xt, 8)
+                    sums.append([F[pl.ds(f * FS + PAD + row, 8), :] for f in range(2)])
+            for i in range(16):
+                coef = [CS[pl.ds((r * 16 + i) * 8, 8), :] for r in range(R)]
+                for xt in range(XT):
+                    row = pl.multiple_of(((i % R) * NZ + z) * BX + 8 * xt, 8)
+                    basis = F[pl.ds((i // R + 1) * FS + PAD + row, 8), :]
+                    image = W[pl.ds((i // R) * FR + row, 8), :]
+                    for r in range(R):
+                        both = sums[r * XT + xt]
+                        both[0] = both[0] + coef[r] * basis
+                        both[1] = both[1] - coef[r] * image
+            for r in range(R):
+                for xt in range(XT):
+                    sol[r, z, pl.ds(8 * xt, 8), :] = sums[r * XT + xt][0]
+                    res[r, z, pl.ds(8 * xt, 8), :] = sums[r * XT + xt][1]
+            return carry
+
+        lax.fori_loop(0, planes, plane, 0)
+        for copy in writes(step):
+            copy.start()
         return carry
 
-    lax.fori_loop(0, planes, body, 0)
-
-
-UPDATE_STEPS = 4
+    lax.fori_loop(0, UPDATE_STEPS, body, 0)
+    for step in range(UPDATE_STEPS):
+        for copy in writes(step):
+            copy.wait()
 
 
 def on_device(gx_size, gy_size, right_side, start_field, center, weights):
@@ -504,6 +514,7 @@
     f32 = jnp.float32
     flat = lambda a: a.reshape(-1, L)
     held = pltpu.MemorySpace.VMEM
+    rows_for = lambda devices: 8 + (2 * devices + 5) // 8 * 8
     shape = lambda *dims: jax.ShapeDtypeStruct(dims, f32)
     in_hbm = lambda a: pltpu.with_memory_space_constraint(flat(a), pltpu.HBM)
     fields, images, coeffs = pl.pallas_call(
@@ -521,11 +532,11 @@
             pltpu.VMEM((5, 2, 2, BX, L), f32),
             pltpu.VMEM((5, 2, 2, R * HALF, L), f32),
             pltpu.VMEM((5, 2, BX, L), f32),
-            pltpu.VMEM((BX, L), f32),
             pltpu.VMEM((2 * 2 * GROUP * R * XT * 8, L), f32),
+            pltpu.VMEM((8 * USED, L), f32),
             pltpu.VMEM((LANES, L), f32),
-            pltpu.VMEM((inner, 8, LANES), f32),
-            pltpu.VMEM((outer * gy_size, 8, LANES), f32),
+            pltpu.VMEM((rows_for(inner), L), f32),
+            pltpu.VMEM((rows_for(outer * gy_size), L), f32),
             dma((4, 6)),
             dma((5, 2, 2)), dma((5, 2, 2)), dma((5, 2, 2)), dma((5, 2, 2)),
             dma((inner,)), dma((inner,)),
@@ -535,15 +546,14 @@
             collective_id=0, has_side_effects=True, vmem_limit_bytes=32 * 1024 * 1024,
         ),
     )(in_hbm(right_side), in_hbm(start_field), in_hbm(center), in_hbm(weights))
-    block = pl.BlockSpec((R, NZ // UPDATE_STEPS, BX, L), lambda i: (0, i, 0, 0))
     return pl.pallas_call(
         update,
-        grid=(UPDATE_STEPS,),
         out_shape=[shape(R, NZ, BX, L)] * 2,
-        in_specs=[pl.BlockSpec(memory_space=held)] * 3 + [block],
-        out_specs=[block, block],
-        compiler_params=pltpu.CompilerParams(vmem_limit_bytes=24 * 1024 * 1024),
-    )(fields, images, coeffs, pltpu.with_memory_space_constraint(start_field, pltpu.HBM))
+        in_specs=[pl.BlockSpec(memory_space=held)] * 3,
+        out_specs=[pl.BlockSpec(memory_space=pltpu.HBM)] * 2,
+        scratch_shapes=[pltpu.VMEM((R, NZ, BX, L), f32)] * 2 + [dma((2, UPDATE_STEPS))],
+        compiler_params=pltpu.CompilerParams(vmem_limit_bytes=16 * 1024 * 1024),
+    )(fields, images, coeffs)
 
 
 def solution(mesh):

time: 48.3 us -> 44.7 us (0.925)
  Pallas kernels: 47.5 us -> 44 us
    pallas_call x1, Pallas kernels: 42.1 us -> 39.7 us  [on_device(): pl.pallas_call(functools.partial(kernel, gx_size, gy_size, inner), out_sh...]
    pallas_call x1, Pallas kernels: 5.36 us -> 4.25 us  [on_device(): pl.pallas_call(update, out_shape=[shape(R, NZ, BX, L)] * 2, in_specs=[pl....]
where the time goes in v2:
time: 44.7 us; the launch traced here: 44.6 us
  Pallas kernels  44 us (98%)
  between operations  0.64 us (1%)
    pallas_call x1, Pallas kernels, on_device(): pl.pallas_call(functools.partial(kernel, gx_size, gy_size, inner), out_sh...  39.7 us
    pallas_call x1, Pallas kernels, on_device(): pl.pallas_call(update, out_shape=[shape(R, NZ, BX, L)] * 2, in_specs=[pl....  4.25 us

profile of v2, /device:TPU:1, one launch (start us, length us, event | category | flops | bytes accessed | tf_op | source)
XLA Modules:
  0.0 44.6 jit_solution(13832746265548725095)
XLA Ops:
  0.6 39.7 %shard_map.59 = (f32[11760,128]{1,0:T(8,128)S(1)}, f32[9216,128]{1,0:T(8,128)S(1)}, f32[512,128]{1,0:T(8,128)S(1)}) custom-call(f32[2304,128]{1,0:T(8,128)} %bitcast.5, f32[2304,128]{1,0:T(8,128)} %bitcast.6, f32[576,128]{1,0:T(8,128)} %bitcast.7, f32[3456,128]{1,0:T(8,128)} %bitcast.4), custom_call_target="tpu_custom_call" | custom-call | tf_op jit(solution)/shard_map/pallas_call | solution.py:520
  40.4 4.2 %shard_map.60 = (f32[4,24,24,128]{3,2,1,0:T(8,128)}, f32[4,24,24,128]{3,2,1,0:T(8,128)}) custom-call(f32[11760,128]{1,0:T(8,128)S(1)} %get-tuple-element.5.F, f32[9216,128]{1,0:T(8,128)S(1)} %get-tuple-element.6.W, f32[512,128]{1,0:T(8,128)S(1)} %get-tuple-element.7.CS), custom_call_target="tpu_custom_call" | custom-call | tf_op jit(solution)/shard_map/pallas_call | solution.py:549

commit v3 on v2

--- a/solution.py
+++ b/solution.py
@@ -98,16 +98,6 @@
             F[pl.ds(f * FS + 8 * p, 8), :] = zero
             F[pl.ds(f * FS + PAD + FR + 8 * p, 8), :] = zero
 
-    for cond, ref, side in (
-        (first_x, HX, 0), (last_x, HX, 1), (first_y, HY, 0), (last_y, HY, 1),
-    ):
-        @pl.when(cond)
-        def _(ref=ref, side=side):
-            for level in range(5):
-                for half in range(2):
-                    for q in range(ref.shape[3] // 8):
-                        ref[level, half, side, pl.ds(8 * q, 8), :] = zero
-
     tiles = [(xt, r) for xt in range(XT) for r in range(R)]
 
     def tile_row(r, z, xt):
@@ -124,44 +114,45 @@
         mask = ((lane + (1 - j2)) & (L - 1)) < 2
         return jnp.where(mask, pltpu.roll(tile, j2, 1), acc)
 
-    def copies(level, half):
-        result = []
-        for missing, lands, takes, gap, row in (
-            (last_x, 0, 1, (gx + 1, gy), XS), (first_x, 1, 0, (gx - 1, gy), XS),
-            (last_y, 0, None, (gx, gy + 1), YS), (first_y, 1, None, (gx, gy - 1), YS),
-        ):
-            along_x = row is XS
-            source = XS.at[level, half, takes] if along_x else YS.at[level, half]
-            target = (HX if along_x else HY).at[level, half, lands]
-            out_sem, in_sem = (sx, rx) if along_x else (sy, ry)
-            result.append((missing, pltpu.make_async_remote_copy(
-                src_ref=source, dst_ref=target,
-                send_sem=out_sem.at[level, half, lands], recv_sem=in_sem.at[level, half, lands],
-                device_id=gap, device_id_type=MESH)))
-        return result
-
-    def send(level, half, acc):
+    up_x, down_x = (lax.rem(gx + 1, gx_size), gy), (lax.rem(gx + gx_size - 1, gx_size), gy)
+    up_y, down_y = (gx, lax.rem(gy + 1, gy_size)), (gx, lax.rem(gy + gy_size - 1, gy_size))
+
+    def copies_x(level, half):
+        return [
+            pltpu.make_async_remote_copy(
+                src_ref=XS.at[level, half, 1 - lands], dst_ref=HX.at[level, half, lands],
+                send_sem=sx.at[level, half, lands], recv_sem=rx.at[level, half, lands],
+                device_id=peer, device_id_type=MESH)
+            for lands, peer in enumerate((up_x, down_x))
+        ]
+
+    def copies_y(level, half):
+        return [
+            pltpu.make_async_remote_copy(
+                src_ref=YS.at[level, half], dst_ref=HY.at[level, half, lands],
+                send_sem=sy.at[level, half, lands], recv_sem=ry.at[level, half, lands],
+                device_id=peer, device_id_type=MESH)
+            for lands, peer in enumerate((up_y, down_y))
+        ]
+
+    def send_x(level, half):
+        for copy in copies_x(level, half):
+            copy.start()
+
+    def send_y(level, half, acc):
         for xt in range(XT):
             YS[level, half, pl.ds(8 * xt, 8), :] = acc[xt]
-        for missing, copy in copies(level, half):
-            @pl.when(jnp.logical_not(missing))
-            def _(copy=copy):
-                copy.start()
+        for copy in copies_y(level, half):
+            copy.start()
 
     def receive(level, half):
-        for missing, (_, copy) in zip(
-            (first_x, last_x, first_y, last_y), copies(level, half)
-        ):
-            @pl.when(jnp.logical_not(missing))
-            def _(copy=copy):
-                copy.wait_recv()
+        for copy in copies_y(level, half) + copies_x(level, half):
+            copy.wait_recv()
 
     def sent(level):
         for half in range(2):
-            for missing, copy in copies(level, half):
-                @pl.when(jnp.logical_not(missing))
-                def _(copy=copy):
-                    copy.wait_send()
+            for copy in copies_x(level, half) + copies_y(level, half):
+                copy.wait_send()
 
     slot = 2 * GROUP * R * XT * 8
 
@@ -261,10 +252,9 @@
             )
             for xt in range(XT)
         ]
-        acc = [zero] * XT
-        for zh in range(HALF):
+        def plane(zh, xt):
             z = half * HALF + zh
-            for xt, r in tiles:
+            for r in range(R):
                 row = tile_row(r, z, xt)
                 halo = pltpu.roll(halos[xt], (L - pack_lane(r, zh)) % L, 1)
                 image = W[pl.ds(out + row, 8), :] - WE[pl.ds(z * BX + 8 * xt, 8), :] * halo
@@ -288,10 +278,24 @@
                             XS[level + 1, half, side, pl.ds(r * HALF + zh, 1), :] = (
                                 following[take : take + 1]
                             )
-                    acc[xt] = pack_tile(following, r, zh, acc[xt])
+
+        for zh in range(HALF):
+            plane(zh, 0)
+            plane(zh, XT - 1)
+        if level < 4:
+            send_x(level + 1, half)
+        for zh in range(HALF):
+            for xt in range(1, XT - 1):
+                plane(zh, xt)
+        if level < 4:
+            acc = [zero] * XT
+            for zh in range(HALF):
+                for xt, r in tiles:
+                    row = tile_row(r, half * HALF + zh, xt)
+                    acc[xt] = pack_tile(F[pl.ds(ahead + row, 8), :], r, zh, acc[xt])
+            send_y(level + 1, half, acc)
         if half and level < 4:
             first_rolls(level + 1)
-        return acc
 
     def combine(a, b, d):
         mask = (sub & d) == 0
@@ -333,7 +337,8 @@
         packed.append(lax.fori_loop(0, HALF // GROUP, pack_body, (zero,) * XT))
     pl.semaphore_wait(barrier, len(hello) + len(inner_peers) + len(outer_peers))
     for half in range(2):
-        send(0, half, packed[half])
+        send_x(0, half)
+        send_y(0, half, packed[half])
 
     for copy in loads[1] + loads[2]:
         copy.wait()
@@ -343,15 +348,18 @@
         for xt in range(XT):
             row = pl.multiple_of(z * BX + 8 * xt, 8)
             stores.append((C6, row, C6[pl.ds(row, 8), :] + 6.0))
-            for side, where, inside in ((0, 0, sub != 0), (1, XT - 1, sub != 7)):
+            for side, where, inside, ends in (
+                (0, 0, sub != 0, first_x), (1, XT - 1, sub != 7, last_x)
+            ):
                 if xt == where:
                     w = WM[pl.ds(side * WR + row, 8), :]
                     stores.append((WM, side * WR + row, jnp.where(inside, w, 0.0)))
                     at = pl.multiple_of((side * NZ + z) * 8, 8)
-                    stores.append((WX, at, jnp.where(inside, 0.0, w)))
+                    stores.append((WX, at, jnp.where(inside | ends, 0.0, w)))
             low = WM[pl.ds(2 * WR + row, 8), :]
             high = WM[pl.ds(3 * WR + row, 8), :]
-            edge = jnp.where(lane == 0, low, jnp.where(lane == L - 1, high, 0.0))
+            edge = jnp.where((lane == 0) & jnp.logical_not(first_y), low, 0.0)
+            edge = jnp.where((lane == L - 1) & jnp.logical_not(last_y), high, edge)
             stores.append((WE, row, edge))
             stores.append((WM, 2 * WR + row, jnp.where(lane == 0, 0.0, low)))
             stores.append((WM, 3 * WR + row, jnp.where(lane == L - 1, 0.0, high)))
@@ -370,9 +378,7 @@
     for level in range(5):
         for half in range(2):
             receive(level, half)
-            acc = correct(level, half)
-            if level < 4:
-                send(level + 1, half, acc)
+            correct(level, half)
         if level < 4:
             bulk(level + 1, level - 1)
         sent(level)

time: 44.7 us -> 45.8 us (1.025)
  Pallas kernels: 44 us -> 45.1 us
    pallas_call x1, Pallas kernels: 39.7 us -> 40.8 us  [on_device(): pl.pallas_call(functools.partial(kernel, gx_size, gy_size, inner), out_sh...]
where the time goes in v3:
time: 45.8 us; the launch traced here: 45.7 us
  Pallas kernels  45.1 us (98%)
  between operations  0.64 us (1%)
    pallas_call x1, Pallas kernels, on_device(): pl.pallas_call(functools.partial(kernel, gx_size, gy_size, inner), out_sh...  40.8 us
    pallas_call x1, Pallas kernels, on_device(): pl.pallas_call(update, out_shape=[shape(R, NZ, BX, L)] * 2, in_specs=[pl....  4.25 us

profile of v3, /device:TPU:1, one launch (start us, length us, event | category | flops | bytes accessed | tf_op | source)
XLA Modules:
  0.0 45.7 jit_solution(10328923753715033898)
XLA Ops:
  0.6 40.8 %shard_map.59 = (f32[11760,128]{1,0:T(8,128)S(1)}, f32[9216,128]{1,0:T(8,128)S(1)}, f32[512,128]{1,0:T(8,128)S(1)}) custom-call(f32[2304,128]{1,0:T(8,128)} %bitcast.5, f32[2304,128]{1,0:T(8,128)} %bitcast.6, f32[576,128]{1,0:T(8,128)} %bitcast.7, f32[3456,128]{1,0:T(8,128)} %bitcast.4), custom_call_target="tpu_custom_call" | custom-call | tf_op jit(solution)/shard_map/pallas_call | solution.py:526
  41.5 4.2 %shard_map.60 = (f32[4,24,24,128]{3,2,1,0:T(8,128)}, f32[4,24,24,128]{3,2,1,0:T(8,128)}) custom-call(f32[11760,128]{1,0:T(8,128)S(1)} %get-tuple-element.5.F, f32[9216,128]{1,0:T(8,128)S(1)} %get-tuple-element.6.W, f32[512,128]{1,0:T(8,128)S(1)} %get-tuple-element.7.CS), custom_call_target="tpu_custom_call" | custom-call | tf_op jit(solution)/shard_map/pallas_call | solution.py:555

commit v4 on v3

--- a/solution.py
+++ b/solution.py
@@ -98,6 +98,16 @@
             F[pl.ds(f * FS + 8 * p, 8), :] = zero
             F[pl.ds(f * FS + PAD + FR + 8 * p, 8), :] = zero
 
+    for cond, ref, side in (
+        (first_x, HX, 0), (last_x, HX, 1), (first_y, HY, 0), (last_y, HY, 1),
+    ):
+        @pl.when(cond)
+        def _(ref=ref, side=side):
+            for level in range(5):
+                for half in range(2):
+                    for q in range(ref.shape[3] // 8):
+                        ref[level, half, side, pl.ds(8 * q, 8), :] = zero
+
     tiles = [(xt, r) for xt in range(XT) for r in range(R)]
 
     def tile_row(r, z, xt):
@@ -136,23 +146,35 @@
         ]
 
     def send_x(level, half):
-        for copy in copies_x(level, half):
-            copy.start()
+        for missing, copy in zip((last_x, first_x), copies_x(level, half)):
+            @pl.when(jnp.logical_not(missing))
+            def _(copy=copy):
+                copy.start()
 
     def send_y(level, half, acc):
         for xt in range(XT):
             YS[level, half, pl.ds(8 * xt, 8), :] = acc[xt]
-        for copy in copies_y(level, half):
-            copy.start()
+        for missing, copy in zip((last_y, first_y), copies_y(level, half)):
+            @pl.when(jnp.logical_not(missing))
+            def _(copy=copy):
+                copy.start()
 
     def receive(level, half):
-        for copy in copies_y(level, half) + copies_x(level, half):
-            copy.wait_recv()
+        for missing, copy in zip(
+            (first_y, last_y, first_x, last_x), copies_y(level, half) + copies_x(level, half)
+        ):
+            @pl.when(jnp.logical_not(missing))
+            def _(copy=copy):
+                copy.wait_recv()
 
     def sent(level):
         for half in range(2):
-            for copy in copies_x(level, half) + copies_y(level, half):
-                copy.wait_send()
+            for missing, copy in zip(
+                (last_x, first_x, last_y, first_y), copies_x(level, half) + copies_y(level, half)
+            ):
+                @pl.when(jnp.logical_not(missing))
+                def _(copy=copy):
+                    copy.wait_send()
 
     slot = 2 * GROUP * R * XT * 8
 

time: 45.8 us -> 42.8 us (0.934)
  Pallas kernels: 45.1 us -> 42 us
    pallas_call x1, Pallas kernels: 40.8 us -> 37.8 us  [on_device(): pl.pallas_call(functools.partial(kernel, gx_size, gy_size, inner), out_sh...]
where the time goes in v4:
time: 42.8 us; the launch traced here: 42.7 us
  Pallas kernels  42 us (98%)
  between operations  0.64 us (1%)
    pallas_call x1, Pallas kernels, on_device(): pl.pallas_call(functools.partial(kernel, gx_size, gy_size, inner), out_sh...  37.8 us
    pallas_call x1, Pallas kernels, on_device(): pl.pallas_call(update, out_shape=[shape(R, NZ, BX, L)] * 2, in_specs=[pl....  4.25 us

profile of v4, /device:TPU:1, one launch (start us, length us, event | category | flops | bytes accessed | tf_op | source)
XLA Modules:
  0.0 42.7 jit_solution(17660567179240029551)
XLA Ops:
  0.6 37.8 %shard_map.59 = (f32[11760,128]{1,0:T(8,128)S(1)}, f32[9216,128]{1,0:T(8,128)S(1)}, f32[512,128]{1,0:T(8,128)S(1)}) custom-call(f32[2304,128]{1,0:T(8,128)} %bitcast.5, f32[2304,128]{1,0:T(8,128)} %bitcast.6, f32[576,128]{1,0:T(8,128)} %bitcast.7, f32[3456,128]{1,0:T(8,128)} %bitcast.4), custom_call_target="tpu_custom_call" | custom-call | tf_op jit(solution)/shard_map/pallas_call | solution.py:548
  38.4 4.2 %shard_map.60 = (f32[4,24,24,128]{3,2,1,0:T(8,128)}, f32[4,24,24,128]{3,2,1,0:T(8,128)}) custom-call(f32[11760,128]{1,0:T(8,128)S(1)} %get-tuple-element.5.F, f32[9216,128]{1,0:T(8,128)S(1)} %get-tuple-element.6.W, f32[512,128]{1,0:T(8,128)S(1)} %get-tuple-element.7.CS), custom_call_target="tpu_custom_call" | custom-call | tf_op jit(solution)/shard_map/pallas_call | solution.py:577

commit v5 on v4

--- a/solution.py
+++ b/solution.py
@@ -77,14 +77,14 @@
         hello.append((lax.rem(gx + step, gx_size), gy))
     for step in (1, gy_size - 1):
         hello.append((gx, lax.rem(gy + step, gy_size)))
-    inner_peers = [(base_x + lax.rem(in_x + i, inner), gy) for i in range(1, inner)]
+    far = lambda step, size: -min(step, size - step)
+    inner_steps = sorted(range(1, inner), key=lambda i: far(i, inner))
+    inner_peers = [(base_x + lax.rem(in_x + i, inner), gy) for i in inner_steps]
     outer_peers = []
-    for i in range(outer):
-        for j in range(gy_size):
-            if i or j:
-                outer_peers.append(
-                    (lax.rem(gx + i * inner, gx_size), lax.rem(gy + j, gy_size))
-                )
+    outer_steps = [(i, j) for i in range(outer) for j in range(gy_size) if i or j]
+    outer_steps.sort(key=lambda s: far(s[0], outer) + far(s[1], gy_size))
+    for i, j in outer_steps:
+        outer_peers.append((lax.rem(gx + i * inner, gx_size), lax.rem(gy + j, gy_size)))
     for peer in hello + inner_peers + outer_peers:
         pl.semaphore_signal(barrier, inc=1, device_id=peer, device_id_type=MESH)
 
@@ -159,10 +159,14 @@
             def _(copy=copy):
                 copy.start()
 
-    def receive(level, half):
-        for missing, copy in zip(
-            (first_y, last_y, first_x, last_x), copies_y(level, half) + copies_x(level, half)
-        ):
+    def receive_x(level, half):
+        for missing, copy in zip((first_x, last_x), copies_x(level, half)):
+            @pl.when(jnp.logical_not(missing))
+            def _(copy=copy):
+                copy.wait_recv()
+
+    def receive_y(level, half):
+        for missing, copy in zip((first_y, last_y), copies_y(level, half)):
             @pl.when(jnp.logical_not(missing))
             def _(copy=copy):
                 copy.wait_recv()
@@ -265,6 +269,7 @@
     def correct(level, half):
         out = max(level - 1, 0) * FR
         ahead = (level + 1) * FS + PAD
+        receive_y(level, half)
         even = (lane & 1) == 0
         halos = [
             jnp.where(
@@ -274,41 +279,51 @@
             )
             for xt in range(XT)
         ]
-        def plane(zh, xt):
+        def columns(zh, xt, r):
             z = half * HALF + zh
-            for r in range(R):
-                row = tile_row(r, z, xt)
-                halo = pltpu.roll(halos[xt], (L - pack_lane(r, zh)) % L, 1)
-                image = W[pl.ds(out + row, 8), :] - WE[pl.ds(z * BX + 8 * xt, 8), :] * halo
-                for side, where in ((0, 0), (1, XT - 1)):
-                    if xt == where:
-                        edge_x = WX[pl.ds((side * NZ + z) * 8, 8), :]
-                        halo_x = HX[level, half, side, pl.ds(r * HALF + zh, 1), :]
-                        image = image - edge_x * jnp.broadcast_to(halo_x, (8, L))
-                if level == 0:
-                    following = B[pl.ds(row, 8), :] - image
-                else:
-                    W[pl.ds(out + row, 8), :] = image
-                    held = F[pl.ds(level * FS + PAD + row, 8), :]
-                    following = image * (1.0 / SCALE_DOWN) - held * (
-                        SHIFTS[level - 1] / SCALE_DOWN
-                    )
-                if level < 4:
-                    F[pl.ds(ahead + row, 8), :] = following
-                    for side, where, take in ((0, 0, 0), (1, XT - 1, 7)):
-                        if xt == where:
-                            XS[level + 1, half, side, pl.ds(r * HALF + zh, 1), :] = (
-                                following[take : take + 1]
-                            )
+            halo = pltpu.roll(halos[xt], (L - pack_lane(r, zh)) % L, 1)
+            edge = WE[pl.ds(z * BX + 8 * xt, 8), :]
+            return W[pl.ds(out + tile_row(r, z, xt), 8), :] - edge * halo
+
+        def finish(zh, xt, r, image):
+            row = tile_row(r, half * HALF + zh, xt)
+            if level == 0:
+                following = B[pl.ds(row, 8), :] - image
+            else:
+                W[pl.ds(out + row, 8), :] = image
+                held = F[pl.ds(level * FS + PAD + row, 8), :]
+                following = image * (1.0 / SCALE_DOWN) - held * (
+                    SHIFTS[level - 1] / SCALE_DOWN
+                )
+            if level < 4:
+                F[pl.ds(ahead + row, 8), :] = following
+            return following
 
         for zh in range(HALF):
-            plane(zh, 0)
-            plane(zh, XT - 1)
+            for xt in (0, XT - 1):
+                for r in range(R):
+                    row = tile_row(r, half * HALF + zh, xt)
+                    W[pl.ds(out + row, 8), :] = columns(zh, xt, r)
+        for zh in range(HALF):
+            for xt in range(1, XT - 1):
+                for r in range(R):
+                    finish(zh, xt, r, columns(zh, xt, r))
+        receive_x(level, half)
+        for zh in range(HALF):
+            z = half * HALF + zh
+            for side, xt, take in ((0, 0, 0), (1, XT - 1, 7)):
+                edge = WX[pl.ds((side * NZ + z) * 8, 8), :]
+                for r in range(R):
+                    halo = HX[level, half, side, pl.ds(r * HALF + zh, 1), :]
+                    image = W[pl.ds(out + tile_row(r, z, xt), 8), :]
+                    image = image - edge * jnp.broadcast_to(halo, (8, L))
+                    following = finish(zh, xt, r, image)
+                    if level < 4:
+                        XS[level + 1, half, side, pl.ds(r * HALF + zh, 1), :] = (
+                            following[take : take + 1]
+                        )
         if level < 4:
             send_x(level + 1, half)
-        for zh in range(HALF):
-            for xt in range(1, XT - 1):
-                plane(zh, xt)
         if level < 4:
             acc = [zero] * XT
             for zh in range(HALF):
@@ -399,7 +414,6 @@
         copy.wait()
     for level in range(5):
         for half in range(2):
-            receive(level, half)
             correct(level, half)
         if level < 4:
             bulk(level + 1, level - 1)
@@ -412,6 +426,8 @@
         jnp.ones((8, L), jnp.float32), RED[...], (((1,), (1,)), ((), ())),
         precision=lax.Precision.HIGHEST, preferred_element_type=jnp.float32,
     )
+
+    pending = []
 
     def exchange(total, buffer, peers, send_sems, recv_sems):
         buffer[pl.ds(0, 8), :] = total
@@ -437,8 +453,7 @@
                 parts[k] + parts[k + 1] if k + 1 < len(parts) else parts[k]
                 for k in range(0, len(parts), 2)
             ]
-        for copy in copies:
-            copy.wait_send()
+        pending.extend(copies)
         total = parts[0]
         for d in (2, 4):
             total = total + pltpu.roll(total, d, 0)
@@ -485,6 +500,8 @@
         coeffs[k] = value
         for r in range(R):
             CS[pl.ds((r * order + k) * 8, 8), :] = jnp.broadcast_to(value[r : r + 1], (8, L))
+    for copy in pending:
+        copy.wait_send()
 
 
 UPDATE_STEPS = 8

time: 42.8 us -> 42 us (0.981)
  Pallas kernels: 42 us -> 41.2 us
    pallas_call x1, Pallas kernels: 37.8 us -> 36.9 us  [on_device(): pl.pallas_call(functools.partial(kernel, gx_size, gy_size, inner), out_sh...]
where the time goes in v5:
time: 42 us; the launch traced here: 41.8 us
  Pallas kernels  41.2 us (98%)
  between operations  0.64 us (2%)
    pallas_call x1, Pallas kernels, on_device(): pl.pallas_call(functools.partial(kernel, gx_size, gy_size, inner), out_sh...  36.9 us
    pallas_call x1, Pallas kernels, on_device(): pl.pallas_call(update, out_shape=[shape(R, NZ, BX, L)] * 2, in_specs=[pl....  4.25 us

profile of v5, /device:TPU:1, one launch (start us, length us, event | category | flops | bytes accessed | tf_op | source)
XLA Modules:
  0.0 41.8 jit_solution(6514070998348896801)
XLA Ops:
  0.6 36.9 %shard_map.59 = (f32[11760,128]{1,0:T(8,128)S(1)}, f32[9216,128]{1,0:T(8,128)S(1)}, f32[512,128]{1,0:T(8,128)S(1)}) custom-call(f32[2304,128]{1,0:T(8,128)} %bitcast.5, f32[2304,128]{1,0:T(8,128)} %bitcast.6, f32[576,128]{1,0:T(8,128)} %bitcast.7, f32[3456,128]{1,0:T(8,128)} %bitcast.4), custom_call_target="tpu_custom_call" | custom-call | tf_op jit(solution)/shard_map/pallas_call | solution.py:565
  37.6 4.2 %shard_map.60 = (f32[4,24,24,128]{3,2,1,0:T(8,128)}, f32[4,24,24,128]{3,2,1,0:T(8,128)}) custom-call(f32[11760,128]{1,0:T(8,128)S(1)} %get-tuple-element.5.F, f32[9216,128]{1,0:T(8,128)S(1)} %get-tuple-element.6.W, f32[512,128]{1,0:T(8,128)S(1)} %get-tuple-element.7.CS), custom_call_target="tpu_custom_call" | custom-call | tf_op jit(solution)/shard_map/pallas_call | solution.py:594

commit v6 on v5

--- a/solution.py
+++ b/solution.py
@@ -299,6 +299,7 @@
                 F[pl.ds(ahead + row, 8), :] = following
             return following
 
+        acc = [zero] * XT
         for zh in range(HALF):
             for xt in (0, XT - 1):
                 for r in range(R):
@@ -307,7 +308,9 @@
         for zh in range(HALF):
             for xt in range(1, XT - 1):
                 for r in range(R):
-                    finish(zh, xt, r, columns(zh, xt, r))
+                    following = finish(zh, xt, r, columns(zh, xt, r))
+                    if level < 4:
+                        acc[xt] = pack_tile(following, r, zh, acc[xt])
         receive_x(level, half)
         for zh in range(HALF):
             z = half * HALF + zh
@@ -325,9 +328,10 @@
         if level < 4:
             send_x(level + 1, half)
         if level < 4:
-            acc = [zero] * XT
             for zh in range(HALF):
                 for xt, r in tiles:
+                    if 0 < xt < XT - 1:
+                        continue
                     row = tile_row(r, half * HALF + zh, xt)
                     acc[xt] = pack_tile(F[pl.ds(ahead + row, 8), :], r, zh, acc[xt])
             send_y(level + 1, half, acc)
@@ -417,7 +421,7 @@
             correct(level, half)
         if level < 4:
             bulk(level + 1, level - 1)
-        sent(level)
+            sent(level)
     gram(3)
 
     for q in range(USED, LANES, 8):
@@ -441,6 +445,8 @@
             copy.start()
             copies.append(copy)
         own = jnp.where(sub < 2, total, 0.0)
+        if not pending:
+            sent(4)
         for copy in copies:
             copy.wait_recv()
         parts = [own]

time: 42 us -> 42.2 us (level)
  no operation moved by 1% of the time
where the time goes in v6:
time: 42.2 us; the launch traced here: 42 us
  Pallas kernels  41.4 us (98%)
  between operations  0.64 us (2%)
    pallas_call x1, Pallas kernels, on_device(): pl.pallas_call(functools.partial(kernel, gx_size, gy_size, inner), out_sh...  37.2 us
    pallas_call x1, Pallas kernels, on_device(): pl.pallas_call(update, out_shape=[shape(R, NZ, BX, L)] * 2, in_specs=[pl....  4.25 us

profile of v6, /device:TPU:1, one launch (start us, length us, event | category | flops | bytes accessed | tf_op | source)
XLA Modules:
  0.0 42.0 jit_solution(5689917750637623325)
XLA Ops:
  0.6 37.2 %shard_map.59 = (f32[11760,128]{1,0:T(8,128)S(1)}, f32[9216,128]{1,0:T(8,128)S(1)}, f32[512,128]{1,0:T(8,128)S(1)}) custom-call(f32[2304,128]{1,0:T(8,128)} %bitcast.5, f32[2304,128]{1,0:T(8,128)} %bitcast.6, f32[576,128]{1,0:T(8,128)} %bitcast.7, f32[3456,128]{1,0:T(8,128)} %bitcast.4), custom_call_target="tpu_custom_call" | custom-call | tf_op jit(solution)/shard_map/pallas_call | solution.py:571
  37.8 4.2 %shard_map.60 = (f32[4,24,24,128]{3,2,1,0:T(8,128)}, f32[4,24,24,128]{3,2,1,0:T(8,128)}) custom-call(f32[11760,128]{1,0:T(8,128)S(1)} %get-tuple-element.5.F, f32[9216,128]{1,0:T(8,128)S(1)} %get-tuple-element.6.W, f32[512,128]{1,0:T(8,128)S(1)} %get-tuple-element.7.CS), custom_call_target="tpu_custom_call" | custom-call | tf_op jit(solution)/shard_map/pallas_call | solution.py:600
